TPU v7x, 256 devices: a whole 4x4x8 slice. The times are simulated.
256 devices in a mesh: tm: 64 (over z, y, x_hi), mp: 4 (over x_lo, core).
Axes of the slice: x: 4 (x_hi: 2, x_lo: 2; x = x_hi * 2 + x_lo), y: 4, z: 8, core: 2. Of those that a mesh axis runs over, the one named last changes fastest.
Arguments:
- frames: bfloat16 [262144, 1024], P('tm', 'mp'), may hold values from -6 to 6
- first_factor: bfloat16 [512, 512, 512], P('tm'), may hold values from -0.25 to 0.25
- second_factor: bfloat16 [512, 512, 512], P('tm'), may hold values from -0.25 to 0.25
- gate_weight: bfloat16 [1024, 1024], P(None, 'mp'), may hold values from -0.1875 to 0.1875
- mix_weight: bfloat16 [1024, 1024], P(None, 'mp'), may hold values from -0.1875 to 0.1875
Outputs:
- mixed: bfloat16 [262144, 1024], P('tm', 'mp')
All inputs are finite; a program needn't handle non-finite values.
Results may differ from a plain program's by a relative error of at most 0.0057.
Values may be sent and summed in bfloat16 or wider, within the bound.
A program may use at most 128 MiB of HBM per device.

v0:
```python
import jax
import jax.numpy as jnp
from jax import lax
from jax.sharding import PartitionSpec as P

NB = 512


def channel_fold(weight, piece):
    return jnp.dot(piece, weight, preferred_element_type=jnp.float32)


def on_device(frames, first_factor, second_factor, gate_weight, mix_weight):
    local_blocks = first_factor.shape[0]
    out_local = mix_weight.shape[1]
    width_local = frames.shape[1]
    gate_pre = channel_fold(gate_weight, lax.all_gather(frames, "mp", axis=1, tiled=True))
    gate = jax.nn.sigmoid(gate_pre).reshape(local_blocks, NB, width_local)
    grid = frames.reshape(local_blocks, NB, width_local)
    first = jnp.einsum("bkj,bjc->bkc", first_factor, grid, preferred_element_type=jnp.float32)
    gated = (first * gate).astype(jnp.bfloat16)
    gated_rows = gated.reshape(local_blocks * NB, width_local)
    channel = channel_fold(mix_weight, lax.all_gather(gated_rows, "mp", axis=1, tiled=True))
    channel = channel.astype(jnp.bfloat16).reshape(local_blocks, NB, out_local)
    arrived = lax.all_to_all(channel, "tm", split_axis=1, concat_axis=0, tiled=True)
    second = jnp.einsum(
        "kmi,ikc->mkc", second_factor, arrived, preferred_element_type=jnp.float32
    ).astype(jnp.bfloat16)
    placed = lax.all_to_all(second, "tm", split_axis=0, concat_axis=1, tiled=True)
    return placed.reshape(local_blocks * NB, out_local)


def solution(mesh):
    in_specs = (
        P("tm", "mp"),
        P("tm", None, None),
        P("tm", None, None),
        P(None, "mp"),
        P(None, "mp"),
    )
    out_specs = P("tm", "mp")
    return jax.shard_map(
        on_device, mesh=mesh, in_specs=in_specs, out_specs=out_specs, check_vma=False
    )
```

profile of v0, /device:TPU:1, one launch (start us, length us, event | category | flops | bytes accessed | tf_op | source)
XLA Modules:
  0.0 334.0 jit_solution(3895553839751204563)
XLA Ops:
  6.5 0.0 copy-start
  6.5 0.0 all-gather.3.cloned.1.call-start
  6.5 0.7 all-gather.3.cloned.1.call-update
  7.3 0.0 copy-start.1
  7.3 0.0 all-gather.5.cloned.1.call-start
  7.3 89.9 %all-gather.3.cloned.1.call-done = bf16[4096,1024]{1,0:T(8,128)(2,1)} async-done(((bf16[4096,256]{1,0:T(8,128)(2,1)}), bf16[4096,1024]{1,0:T(8,128)(2,1)}) %all-gather.3.cloned.1.call-update) | async-done | bytes 8388624 | tf_op jit(solution)/shard_map/all_gather | solution.py:17
  97.3 0.0 copy-done
  97.3 0.0 copy-start.2
  97.3 6.0 %fusion.2 = f32[4096,256]{1,0:T(8,128)S(1)} fusion(bf16[4096,1024]{1,0:T(8,128)(2,1)} %all-gather.3.cloned.1.call-done, bf16[1024,256]{1,0:T(8,128)(2,1)S(1)} %copy-done), kind=kOutput, calls=%fused_computation.4 | convolution fusion | flops 2150629376 | bytes 13107200 | tf_op jit(solution)/shard_map/dot_general | solution.py:10
  103.3 0.0 copy-done.1
  103.3 0.0 copy-done.2
  103.3 0.0 copy-start.4
  103.3 2.6 multiply_convert_fusion
  106.0 0.0 all-gather.5.cloned.1.call-update
  106.0 84.9 %all-gather.5.cloned.1.call-done = bf16[4096,1024]{1,0:T(8,128)(2,1)} async-done(((bf16[4096,256]{1,0:T(8,128)(2,1)}), bf16[4096,1024]{1,0:T(8,128)(2,1)}) %all-gather.5.cloned.1.call-update) | async-done | bytes 8388624 | tf_op jit(solution)/shard_map/all_gather | solution.py:23
  190.9 0.0 copy-done.4
  190.9 5.7 %convolution_convert_fusion = bf16[4096,256]{1,0:T(8,128)(2,1)S(1)} fusion(bf16[4096,1024]{1,0:T(8,128)(2,1)} %all-gather.5.cloned.1.call-done, bf16[1024,256]{1,0:T(8,128)(2,1)S(1)} %copy-done.4), kind=kOutput, calls=%fused_computation.3 | convolution fusion | flops 2148532224 | bytes 11010048 | tf_op jit(solution)/shard_map/dot_general | solution.py:10
  196.6 1.2 copy.14
  197.8 0.0 copy-start.3
  197.8 64.0 %all_to_all.33 = bf16[8,512,256]{2,0,1:T(8,128)(2,1)S(1)} all-to-all(bf16[8,512,256]{2,0,1:T(8,128)(2,1)S(1)} %copy.14), channel_id=1, replica_groups=mesh['tm'=64,'mp'=4] {'tm'}, dimensions={1} | all-to-all | bytes 4194304 | tf_op jit(solution)/shard_map/all_to_all | solution.py:25
  261.8 0.7 copy.16
  262.5 0.0 copy-done.3
  262.5 3.0 convert_bitcast_fusion
  265.5 3.3 copy.18
  268.9 56.9 %all_to_all.34 = bf16[512,8,256]{2,1,0:T(8,128)(2,1)S(1)} all-to-all(bf16[512,8,256]{2,1,0:T(8,128)(2,1)S(1)} %copy.18), channel_id=1, replica_groups=mesh['tm'=64,'mp'=4] {'tm'}, dimensions={0} | all-to-all | bytes 4194304 | tf_op jit(solution)/shard_map/all_to_all | solution.py:29
  325.8 1.5 copy.19
Async XLA Ops:
  6.5 90.7 %copy-start = (bf16[1024,256]{1,0:T(8,128)(2,1)S(1)}, bf16[1024,256]{1,0:T(8,128)(2,1)}, u32[]{:S(2)}) copy-start(bf16[1024,256]{1,0:T(8,128)(2,1)} %param.8) | copy-start | bytes 1572868
  6.5 90.7 %all-gather.3.cloned.1.call-start = ((), (), s32[]{:S(2)}) async-start(), calls=%async_computation.2 | async-start | bytes 10485760 | tf_op jit(solution)/shard_map/all_gather | solution.py:17
  7.3 96.1 %copy-start.1 = (bf16[4096,256]{1,0:T(8,128)(2,1)S(1)}, bf16[4096,256]{1,0:T(8,128)(2,1)}, u32[]{:S(2)}) copy-start(bf16[4096,256]{1,0:T(8,128)(2,1)} %param.5) | copy-start | bytes 6291460
  7.3 183.6 %all-gather.5.cloned.1.call-start = ((), (), s32[]{:S(2)}) async-start(), calls=%async_computation.3 | async-start | bytes 10485760 | tf_op jit(solution)/shard_map/all_gather | solution.py:23
  97.3 6.1 %copy-start.2 = (bf16[8,512,512]{2,1,0:T(8,128)(2,1)S(1)}, bf16[8,512,512]{2,1,0:T(8,128)(2,1)}, u32[]{:S(2)}) copy-start(bf16[8,512,512]{2,1,0:T(8,128)(2,1)} %param.6) | copy-start | bytes 12582916
  103.3 87.6 %copy-start.4 = (bf16[1024,256]{1,0:T(8,128)(2,1)S(1)}, bf16[1024,256]{1,0:T(8,128)(2,1)}, u32[]{:S(2)}) copy-start(bf16[1024,256]{1,0:T(8,128)(2,1)} %param.9) | copy-start | bytes 1572868
  197.8 64.7 %copy-start.3 = (bf16[8,512,512]{2,1,0:T(8,128)(2,1)S(1)}, bf16[8,512,512]{2,1,0:T(8,128)(2,1)}, u32[]{:S(2)}) copy-start(bf16[8,512,512]{2,1,0:T(8,128)(2,1)} %param.7) | copy-start | bytes 12582916
Sparse Core Ops, SparseCore 0:
  9.2 88.0 all-gather.2
  106.1 84.7 all-gather.4
where the time goes:
time: 335 us; the launch traced here: 334 us
  waiting for transfers between devices  176 us (53%)
  blocking collectives  121 us (36%)
  matrix products  17.4 us (5%)
  between operations  13.5 us (4%)
  local copies, waits for them, and re-layouts  6.67 us (2%)
    all_gather x1, waiting for transfers between devices, on_device(): lax.all_gather(frames, 'mp', axis=1, tiled=True)  89.9 us
    all_gather x1, waiting for transfers between devices, on_device(): lax.all_gather(gated_rows, 'mp', axis=1, tiled=True)  84.9 us
    all_to_all x1, blocking collectives, on_device(): lax.all_to_all(channel, 'tm', split_axis=1, concat_axis=0, tiled=True)  64 us
    all_to_all x1, blocking collectives, on_device(): lax.all_to_all(second, 'tm', split_axis=0, concat_axis=1, tiled=True)  56.9 us
    dot_general x2, matrix products, channel_fold(): return jnp.dot(piece, weight, preferred_element_type=jnp.float32)  11.8 us
  transfers between devices with their start and end apart: 2, of which 2 were waited for; matrix products, arithmetic and copies ran while one was open for 0% of the time, Pallas kernels for 0%

commit v1 on v0

v1 whole, which is shorter than its diff:
```python
import jax
import jax.numpy as jnp
from jax import lax
from jax.experimental import pallas as pl
from jax.experimental.pallas import tpu as pltpu
from jax.sharding import PartitionSpec as P

MESH = pl.DeviceIdType.MESH
TM, MP = 64, 4
NB, DW = 512, 256
LB = NB // TM
HALF = 128
BF, F32 = jnp.bfloat16, jnp.float32


def partner(tm, u):
    return lax.rem(tm + (u % 8) * 8 + u // 8 % 8, TM)


def kernel(frames, first_factor, second_factor, gate_w, mix_w, out,
           grid, fv, sv, gw, mw, gated, chan, arrived, rows, sums, second,
           local_sem, f_send, f_recv, w_send, w_recv, a_send, a_recv, o_send, o_recv):
    tm, mp = lax.axis_index("tm"), lax.axis_index("mp")

    def columns(q):
        return pl.ds(pl.multiple_of(q * DW, DW), DW)

    def local(src, dst, at):
        return pltpu.make_async_copy(src, dst, local_sem.at[at])

    def remote(src, dst, send, recv, to):
        return pltpu.make_async_remote_copy(
            src_ref=src, dst_ref=dst, send_sem=send, recv_sem=recv, device_id=to, device_id_type=MESH)

    own = [local(frames.at[s * MP + mp], grid.at[s, :, columns(mp)], s) for s in range(2)]
    own += [local(first_factor.at[s * MP + mp], fv.at[s], 2 + s) for s in range(2)]
    own += [local(gate_w, gw.at[mp], 4), local(mix_w, mw.at[mp], 5), local(second_factor, sv, 6)]
    for c in own:
        c.start()

    barrier = pltpu.get_barrier_semaphore()

    def greet(n, _):
        to = lax.rem(tm * MP + mp + n, TM * MP)
        pl.semaphore_signal(barrier, inc=1, device_id=(to // MP, lax.rem(to, MP)), device_id_type=MESH)
        return 0

    lax.fori_loop(1, TM * MP, greet, 0)
    pl.semaphore_wait(barrier, TM * MP - 1)

    def frames_to(s, p):
        to = mp ^ p
        return remote(frames.at[s * MP + to], grid.at[s, :, columns(mp)],
                      f_send.at[s, p - 1], f_recv.at[s, p - 1], (tm, to))

    def weight_moves(w, buf, at):
        far = remote(w, buf.at[mp], w_send.at[at, 0], w_recv.at[at, 0], (tm ^ 1, mp ^ 2))
        near = remote(w, buf.at[mp], w_send.at[at, 1], w_recv.at[at, 1], (tm, mp ^ 1))
        on = remote(buf.at[mp ^ 2], buf.at[mp ^ 2], w_send.at[at, 2], w_recv.at[at, 2], (tm, mp ^ 1))
        return far, near, on

    fr = [[frames_to(s, p) for p in (2, 3, 1)] for s in range(2)]
    gmove, mmove = weight_moves(gate_w, gw, 0), weight_moves(mix_w, mw, 1)
    for c in (fr[0][0], fr[0][1], gmove[0], fr[0][2], gmove[1], mmove[1]):
        c.start()
    gmove[0].wait_recv()
    gmove[2].start()
    gmove[0].wait_send()
    mmove[0].start()
    for c in fr[0]:
        c.wait_send()
    for c in fr[1]:
        c.start()

    def gate_stage(s):
        def part(n, _):
            q, r = n // 2, pl.multiple_of(lax.rem(n, 2) * 256, 256)
            cols = columns(q)
            pre = jnp.dot(grid[s, pl.ds(r, 256), :], gw[q], preferred_element_type=F32)
            mixed = jnp.dot(fv[s, pl.ds(r, 256), :], grid[s, :, cols], preferred_element_type=F32)
            gated[pl.ds(r, 256), cols] = (mixed * jax.nn.sigmoid(pre)).astype(BF)
            return 0

        lax.fori_loop(0, 8, part, 0)

    def mix_stage(s, q):
        def part(n, _):
            r = pl.multiple_of(n * 256, 256)
            y = jnp.dot(gated[pl.ds(r, 256), :], mw[q], preferred_element_type=F32)
            for h in range(2):
                chan[s, q, pl.ds(n * 32, 32), h] = y[:, h * HALF:(h + 1) * HALF].reshape(32, LB, HALF).astype(BF)
            return 0

        lax.fori_loop(0, 2, part, 0)

    def send_whole(q, first):
        def one(u, _):
            to = partner(tm, u)
            remote(chan.at[0, q, to], arrived.at[:, tm, 0, mp], a_send.at[0], a_recv.at[0], (to, q)).start()
            return 0

        lax.fori_loop(first, TM, one, 0)

    def send_half(q, h, first):
        def one(u, _):
            to = partner(tm, u)
            remote(chan.at[1, q, to, h], arrived.at[h, tm, 1, mp], a_send.at[1 + h], a_recv.at[1 + h], (to, q)).start()
            return 0

        lax.fori_loop(first, TM, one, 0)

    for c in fr[0]:
        c.wait_recv()
    gmove[1].wait_recv()
    gmove[2].wait_recv()
    for at in (0, 2, 4):
        own[at].wait()
    gate_stage(0)
    own[5].wait()
    mix_stage(0, mp)
    pltpu.make_async_copy(chan.at[0, mp, tm], arrived.at[:, tm, 0, mp], a_recv.at[0]).start()
    send_whole(mp, 1)
    mmove[1].wait_recv()
    mix_stage(0, mp ^ 1)
    send_whole(mp ^ 1, 0)
    mmove[0].wait_recv()
    mmove[2].start()
    mix_stage(0, mp ^ 2)
    send_whole(mp ^ 2, 0)
    mmove[2].wait_recv()
    mix_stage(0, mp ^ 3)
    send_whole(mp ^ 3, 0)

    for c in fr[1]:
        c.wait_recv()
    for at in (1, 3):
        own[at].wait()
    gate_stage(1)
    for p in range(MP):
        mix_stage(1, mp ^ p)
        if p == 0:
            for h in range(2):
                pltpu.make_async_copy(chan.at[1, mp, tm, h], arrived.at[h, tm, 1, mp], a_recv.at[1 + h]).start()
        send_half(mp ^ p, 0, 1 if p == 0 else 0)
    for p in range(MP):
        send_half(mp ^ p, 1, 1 if p == 0 else 0)

    own[6].wait()
    pltpu.make_async_copy(arrived.at[:, :, 0], arrived.at[:, :, 0], a_recv.at[0]).wait()
    for h in range(2):
        got = arrived.at[h, :, 1]
        pltpu.make_async_copy(got, got, a_recv.at[1 + h]).wait()

        def widen(n, _):
            t = arrived[h, pl.ds(n * 8, 8)]
            rows[pl.ds(pl.multiple_of(n * 512, 512), 512), :] = t.astype(F32).reshape(512, HALF)
            return 0

        lax.fori_loop(0, 8, widen, 0)
        for k in range(LB):
            x = rows[pl.ds(k, NB, stride=LB), :].astype(BF)
            sums[pl.ds(k, NB, stride=LB), :] = jnp.dot(sv[k], x, preferred_element_type=F32)

        def narrow(n, _):
            t = sums[pl.ds(pl.multiple_of(n * 512, 512), 512), :]
            second[h, pl.ds(n * 8, 8)] = t.reshape(8, LB, LB, HALF).astype(BF)
            return 0

        lax.fori_loop(0, 8, narrow, 0)
        half = pl.ds(h * HALF, HALF)
        pltpu.make_async_copy(second.at[h, tm], out.at[:, tm, :, half], o_recv.at[h]).start()

        def place(u, _):
            to = partner(tm, u)
            remote(second.at[h, to], out.at[:, tm, :, half], o_send.at[h], o_recv.at[h], (to, mp)).start()
            return 0

        lax.fori_loop(1, TM, place, 0)

    for c in fr[1]:
        c.wait_send()
    for at in (1, 2):
        gmove[at].wait_send()
    for c in mmove:
        c.wait_send()
    gone = chan.at[0, 0]

    def left(src, sem):
        pltpu.make_async_copy(src, src, sem).wait()

    for p in range(3):
        left(gone, a_send.at[0])
    left(chan.at[0, 0, pl.ds(0, TM - 1)], a_send.at[0])
    for h in range(2):
        for p in range(3):
            left(chan.at[1, 0, :, h], a_send.at[1 + h])
        left(chan.at[1, 0, pl.ds(0, TM - 1), h], a_send.at[1 + h])
        left(second.at[h, pl.ds(0, TM - 1)], o_send.at[h])
        half = pl.ds(h * HALF, HALF)
        left(out.at[:, :, :, half], o_recv.at[h])


def on_device(frames, first_factor, second_factor, gate_w, mix_w):
    frames = frames.reshape(LB, NB, DW)
    out = pl.pallas_call(
        kernel,
        out_shape=jax.ShapeDtypeStruct((LB, TM, LB, DW), BF),
        in_specs=[pl.BlockSpec(memory_space=pl.ANY)] * 5,
        out_specs=pl.BlockSpec(memory_space=pl.ANY),
        scratch_shapes=[
            pltpu.VMEM((2, NB, MP * DW), BF),
            pltpu.VMEM((2, NB, NB), BF),
            pltpu.VMEM((LB, NB, NB), BF),
            pltpu.VMEM((MP, MP * DW, DW), BF),
            pltpu.VMEM((MP, MP * DW, DW), BF),
            pltpu.VMEM((NB, MP * DW), BF),
            pltpu.VMEM((2, MP, TM, 2, LB, HALF), BF),
            pltpu.VMEM((2, TM, 2, MP, LB, HALF), BF),
            pltpu.VMEM((NB * LB, HALF), F32),
            pltpu.VMEM((NB * LB, HALF), F32),
            pltpu.VMEM((2, TM, LB, LB, HALF), BF),
            pltpu.SemaphoreType.DMA((7,)),
            pltpu.SemaphoreType.DMA((2, 3)),
            pltpu.SemaphoreType.DMA((2, 3)),
            pltpu.SemaphoreType.DMA((2, 3)),
            pltpu.SemaphoreType.DMA((2, 3)),
            pltpu.SemaphoreType.DMA((3,)),
            pltpu.SemaphoreType.DMA((3,)),
            pltpu.SemaphoreType.DMA((2,)),
            pltpu.SemaphoreType.DMA((2,)),
        ],
        compiler_params=pltpu.CompilerParams(
            collective_id=0, has_side_effects=True, vmem_limit_bytes=48 << 20),
        cost_estimate=pl.CostEstimate(flops=6_500_000_000, bytes_accessed=16 << 20, transcendentals=1 << 20),
        name="monarch",
    )(frames, first_factor, second_factor, gate_w, mix_w)
    return out.reshape(LB * NB, DW)


def solution(mesh):
    in_specs = (
        P("tm", "mp"),
        P("tm", None, None),
        P("tm", None, None),
        P(None, "mp"),
        P(None, "mp"),
    )
    return jax.shard_map(
        on_device, mesh=mesh, in_specs=in_specs, out_specs=P("tm", "mp"), check_vma=False
    )
```

time: 335 us -> 133 us (0.40)
  waiting for transfers between devices: 176 us -> 0 us
  Pallas kernels: 0 us -> 128 us
  blocking collectives: 121 us -> 0 us
  matrix products: 17.4 us -> 0 us
  between operations: 13.5 us -> 0.01 us
    all_gather x2 -> x0, waiting for transfers between devices: 175 us -> none  [the longest x1 89.9 us: on_device(): lax.all_gather(frames, 'mp', axis=1, tiled=True)]
    pallas_call x0 -> x1, Pallas kernels: none -> 128 us  [on_device(): pl.pallas_call(kernel, out_shape=jax.ShapeDtypeStruct((LB, TM, LB, DW), B...]
    all_to_all x2 -> x0, blocking collectives: 121 us -> none  [the longest x1 64 us: on_device(): lax.all_to_all(channel, 'tm', split_axis=1, concat_axis=0, tiled=True)]
    dot_general x4 -> x0, matrix products: 17.4 us -> none  [the longest x2 11.8 us: channel_fold(): return jnp.dot(piece, weight, preferred_element_type=jnp.float32)]
    unnamed x10 -> x7, local copies, waits for them, and re-layouts: 0.02 us -> 4.99 us
  transfers between devices with their start and end apart: 2 -> 0, of which waited for: 2 -> 0; matrix products, arithmetic and copies ran while one was open for 0% -> 0% of each run, Pallas kernels for 0% -> 0%
where the time goes in v1:
time: 133 us
  Pallas kernels  128 us (96%)
  local copies, waits for them, and re-layouts  4.99 us (4%)
    pallas_call x1, Pallas kernels, on_device(): pl.pallas_call(kernel, out_shape=jax.ShapeDtypeStruct((LB, TM, LB, DW), B...  128 us
    unnamed x7, local copies, waits for them, and re-layouts  4.99 us

profile of v1, /device:TPU:1, one launch (start us, length us, event | category | flops | bytes accessed | tf_op | source)
XLA Modules:
  0.0 133.1 jit_solution(2354516217239025196)
XLA Ops:
  0.0 0.0 copy-start
  0.0 1.6 %copy-done = bf16[4096,256]{1,0:T(8,128)(2,1)S(1)} copy-done((bf16[4096,256]{1,0:T(8,128)(2,1)S(1)}, bf16[4096,256]{1,0:T(8,128)(2,1)}, u32[]{:S(2)}) %copy-start) | copy-done | bytes 2097176
  1.6 0.0 copy-start.1
  1.6 1.0 copy-done.1
  2.6 0.0 copy-start.2
  2.6 1.0 copy-done.2
  3.7 128.1 %monarch.1 = bf16[8,64,8,256]{3,2,1,0:T(8,128)(2,1)S(1)} custom-call(bf16[8,512,256]{2,1,0:T(8,128)(2,1)S(1)} %bitcast.3, bf16[8,512,512]{2,1,0:T(8,128)(2,1)} %first_factor.1, bf16[8,512,512]{2,1,0:T(8,128)(2,1)} %second_factor.1, bf16[1024,256]{1,0:T(8,128)(2,1)S(1)} %copy-done.1, bf16[1024,256]{1,0:T(8,128)(2,1)S(1)} %copy-done.2), custom_call_target="tpu_custom_call" | custom-call | flops 6499999744 | bytes 16777216 | tf_op jit(solution)/shard_map/monarch/pallas_call | solution.py:205
  131.8 1.3 copy.7
Async XLA Ops:
  0.0 1.6 %copy-start = (bf16[4096,256]{1,0:T(8,128)(2,1)S(1)}, bf16[4096,256]{1,0:T(8,128)(2,1)}, u32[]{:S(2)}) copy-start(bf16[4096,256]{1,0:T(8,128)(2,1)} %param.5) | copy-start | bytes 6291460
  1.6 1.0 copy-start.1
  2.6 1.0 copy-start.2

commit v2 on v1

--- a/solution.py
+++ b/solution.py
@@ -19,7 +19,7 @@
 
 def kernel(frames, first_factor, second_factor, gate_w, mix_w, out,
            grid, fv, sv, gw, mw, gated, chan, arrived, rows, sums, second,
-           local_sem, f_send, f_recv, w_send, w_recv, a_send, a_recv, o_send, o_recv):
+           local_sem, f_send, f_recv, w_send, w_recv, a_send, a_recv, o_send, o_recv, in_sem):
     tm, mp = lax.axis_index("tm"), lax.axis_index("mp")
 
     def columns(q):
@@ -38,15 +38,27 @@
     for c in own:
         c.start()
 
+    z, y, x = tm // 8, tm // 2 % 4, lax.rem(tm, 2) * MP + mp
+
+    def along_x(sem):
+        for n in range(1, 8):
+            to = x ^ n
+            pl.semaphore_signal(sem, inc=1, device_id=(tm // 2 * 2 + to // MP, lax.rem(to, MP)), device_id_type=MESH)
+
+    def along_y(sem):
+        for n in range(1, 4):
+            to = z * 8 + lax.rem(y + n, 4) * 2 + lax.rem(tm, 2)
+            pl.semaphore_signal(sem, inc=1, device_id=(to, mp), device_id_type=MESH)
+
+    def along_z(sem):
+        for n in range(1, 8):
+            pl.semaphore_signal(sem, inc=1, device_id=(lax.rem(tm + n * 8, TM), mp), device_id_type=MESH)
+
     barrier = pltpu.get_barrier_semaphore()
-
-    def greet(n, _):
-        to = lax.rem(tm * MP + mp + n, TM * MP)
-        pl.semaphore_signal(barrier, inc=1, device_id=(to // MP, lax.rem(to, MP)), device_id_type=MESH)
-        return 0
-
-    lax.fori_loop(1, TM * MP, greet, 0)
-    pl.semaphore_wait(barrier, TM * MP - 1)
+    along_x(barrier)
+    along_y(barrier)
+    along_z(barrier)
+    pl.semaphore_wait(barrier, 17)
 
     def frames_to(s, p):
         to = mp ^ p
@@ -63,6 +75,10 @@
     gmove, mmove = weight_moves(gate_w, gw, 0), weight_moves(mix_w, mw, 1)
     for c in (fr[0][0], fr[0][1], gmove[0], fr[0][2], gmove[1], mmove[1]):
         c.start()
+    along_y(in_sem.at[0])
+    pl.semaphore_wait(in_sem.at[0], 3)
+    along_z(in_sem.at[1])
+    pl.semaphore_wait(in_sem.at[1], 7)
     gmove[0].wait_recv()
     gmove[2].start()
     gmove[0].wait_send()
@@ -204,8 +220,8 @@
     frames = frames.reshape(LB, NB, DW)
     out = pl.pallas_call(
         kernel,
-        out_shape=jax.ShapeDtypeStruct((LB, TM, LB, DW), BF),
-        in_specs=[pl.BlockSpec(memory_space=pl.ANY)] * 5,
+        out_shape=pltpu.VMEM((LB, TM, LB, DW), BF),
+        in_specs=[pl.BlockSpec(memory_space=pltpu.HBM)] * 5,
         out_specs=pl.BlockSpec(memory_space=pl.ANY),
         scratch_shapes=[
             pltpu.VMEM((2, NB, MP * DW), BF),
@@ -228,9 +244,10 @@
             pltpu.SemaphoreType.DMA((3,)),
             pltpu.SemaphoreType.DMA((2,)),
             pltpu.SemaphoreType.DMA((2,)),
+            pltpu.SemaphoreType.REGULAR((2,)),
         ],
         compiler_params=pltpu.CompilerParams(
-            collective_id=0, has_side_effects=True, vmem_limit_bytes=48 << 20),
+            collective_id=0, has_side_effects=True, vmem_limit_bytes=56 << 20),
         cost_estimate=pl.CostEstimate(flops=6_500_000_000, bytes_accessed=16 << 20, transcendentals=1 << 20),
         name="monarch",
     )(frames, first_factor, second_factor, gate_w, mix_w)

time: 133 us -> 124 us (0.932); the launches traced: 133 us -> 123 us
  Pallas kernels: 128 us -> 121 us
  local copies, waits for them, and re-layouts: 4.99 us -> 1.32 us
    pallas_call x1, Pallas kernels: 128 us -> 121 us  [on_device(): pl.pallas_call(kernel, out_shape=pltpu.VMEM((LB, TM, LB, DW), BF), in_spe...]
    unnamed x7 -> x1, local copies, waits for them, and re-layouts: 4.99 us -> 1.32 us
where the time goes in v2:
time: 124 us; the launch traced here: 123 us
  Pallas kernels  121 us (98%)
  local copies, waits for them, and re-layouts  1.32 us (1%)
    pallas_call x1, Pallas kernels, on_device(): pl.pallas_call(kernel, out_shape=pltpu.VMEM((LB, TM, LB, DW), BF), in_spe...  121 us

profile of v2, /device:TPU:1, one launch (start us, length us, event | category | flops | bytes accessed | tf_op | source)
XLA Modules:
  0.0 122.7 jit_solution(4517847771459045126)
XLA Ops:
  0.0 121.4 %monarch.1 = bf16[8,64,8,256]{3,2,1,0:T(8,128)(2,1)S(1)} custom-call(bf16[8,512,256]{2,1,0:T(8,128)(2,1)} %bitcast.3, bf16[8,512,512]{2,1,0:T(8,128)(2,1)} %first_factor.1, bf16[8,512,512]{2,1,0:T(8,128)(2,1)} %second_factor.1, bf16[1024,256]{1,0:T(8,128)(2,1)} %gate_w.1, bf16[1024,256]{1,0:T(8,128)(2,1)} %mix_w.1), custom_call_target="tpu_custom_call" | custom-call | flops 6499999744 | bytes 16777216 | tf_op jit(solution)/shard_map/monarch/pallas_call | solution.py:221
  121.4 1.3 %copy.7 = bf16[4096,256]{1,0:T(8,128)(2,1)} copy(bf16[4096,256]{1,0:T(8,128)(2,1)S(1)} %bitcast.2) | data formatting | bytes 4194304

commit v3 on v2

v3 whole, which is shorter than its diff:
```python
import jax
import jax.numpy as jnp
from jax import lax
from jax.experimental import pallas as pl
from jax.experimental.pallas import tpu as pltpu
from jax.sharding import PartitionSpec as P

MESH = pl.DeviceIdType.MESH
TM, MP = 64, 4
NB, DW = 512, 256
LB = NB // TM
HALF = 128
ST = 4
KH, TH = NB // 2, TM // 2
QR = 160
BF, F32 = jnp.bfloat16, jnp.float32


def partner(tm, u):
    return lax.rem(tm + (u % 8) * 8 + u // 8 % 8, TM)


def partner_half(tm, u):
    return lax.rem(tm // 8 + u % 4, 4) * 8 + lax.rem(tm + u // 4, 8)


def kernel(frames, first_factor, second_factor, gate_w, mix_w, out,
           grid, fv, sv, gw, mw, gated, chan, arrived, rows, sums, second,
           local_sem, f_send, f_recv, w_send, w_recv, a_send, a_recv, o_send, o_recv, in_sem):
    tm, mp = lax.axis_index("tm"), lax.axis_index("mp")
    z, y, x = tm // 8, tm // 2 % 4, lax.rem(tm, 2) * MP + mp
    chip = mp // 2
    half_k = lax.rem(mp + z + jnp.where(z < 4, 1, 0), 2)

    def columns(q):
        return pl.ds(pl.multiple_of(q * DW, DW), DW)

    my_k = pl.ds(pl.multiple_of(half_k * KH, KH), KH)

    def local(src, dst, at):
        return pltpu.make_async_copy(src, dst, local_sem.at[at])

    def remote(src, dst, send, recv, to):
        return pltpu.make_async_remote_copy(
            src_ref=src, dst_ref=dst, send_sem=send, recv_sem=recv, device_id=to, device_id_type=MESH)

    own = [local(frames.at[2 * s + chip], grid.at[s, :, columns(mp)], s) for s in range(ST)]
    own += [local(first_factor.at[2 * s + chip, my_k], fv.at[s], ST + s) for s in range(ST)]
    own += [local(gate_w, gw.at[mp], 2 * ST), local(mix_w, mw.at[mp], 2 * ST + 1), local(second_factor, sv, 2 * ST + 2)]
    for c in own:
        c.start()

    def along_x(sem):
        for n in range(1, 8):
            to = x ^ n
            pl.semaphore_signal(sem, inc=1, device_id=(tm // 2 * 2 + to // MP, lax.rem(to, MP)), device_id_type=MESH)

    def along_y(sem):
        for n in range(1, 4):
            to = z * 8 + lax.rem(y + n, 4) * 2 + lax.rem(tm, 2)
            pl.semaphore_signal(sem, inc=1, device_id=(to, mp), device_id_type=MESH)

    def along_z(sem):
        for n in range(1, 8):
            pl.semaphore_signal(sem, inc=1, device_id=(lax.rem(tm + n * 8, TM), mp), device_id_type=MESH)

    barrier = pltpu.get_barrier_semaphore()
    along_x(barrier)
    along_y(barrier)
    along_z(barrier)
    pl.semaphore_wait(barrier, 17)

    other = (tm, mp ^ 1)

    def frame_moves(s):
        cross = remote(frames.at[2 * s + 1 - chip], grid.at[s, :, columns(mp)], f_send.at[s, 0], f_recv.at[s, 0], (tm, mp ^ 2))
        near = remote(frames.at[2 * s + chip], grid.at[s, :, columns(mp)], f_send.at[s, 1], f_recv.at[s, 1], other)
        came = grid.at[s, :, columns(mp ^ 2)]
        return cross, near, remote(came, came, f_send.at[s, 2], f_recv.at[s, 2], other)

    def weight_moves(w, buf, at):
        def move(src, slot, part, kind, to):
            return remote(src.at[part], buf.at[slot, part], w_send.at[at, kind], w_recv.at[at, kind], to)

        def quarter(n):
            return pl.ds(pl.multiple_of(lax.rem(y + 4 - n, 4) * QR, 16), QR)

        held, rest, far = mp ^ 2, pl.ds(4 * QR, MP * DW - 4 * QR), (tm ^ 1, mp ^ 2)
        first, last = move(w, mp, quarter(0), 0, far), move(w, mp, rest, 1, far)
        near = remote(w, buf.at[mp], w_send.at[at, 2], w_recv.at[at, 2], other)
        line = [move(buf.at[held], held, quarter(0), 2 + n,
                     (z * 8 + lax.rem(y + n, 4) * 2 + lax.rem(tm, 2), mp)) for n in range(1, 4)]
        on = [move(buf.at[held], held, quarter(n), 6 + n, other) for n in range(4)]
        on.append(move(buf.at[held], held, rest, 10, other))
        return first, last, near, line, on

    fr = [frame_moves(s) for s in range(ST)]
    gmoves, mmoves = weight_moves(gate_w, gw, 0), weight_moves(mix_w, mw, 1)
    gfirst, glast, gnear, gline, gon = gmoves
    mfirst, mlast, mnear, mline, mon = mmoves
    for c in (gfirst, fr[0][0], fr[0][1], gnear, mnear):
        c.start()
    along_y(in_sem.at[0])
    pl.semaphore_wait(in_sem.at[0], 3)
    along_z(in_sem.at[1])
    gfirst.wait_recv()
    for c in (*gline, gon[0]):
        c.start()
    gfirst.wait_send()
    glast.start()
    pl.semaphore_wait(in_sem.at[1], 7)

    def gate_part(s, q):
        cols = columns(q)
        pre = jnp.dot(grid[s, my_k, :], gw[q], preferred_element_type=F32)
        mixed = jnp.dot(fv[s], grid[s, :, cols], preferred_element_type=F32)
        gated[s, :, cols] = (mixed * jax.nn.sigmoid(pre)).astype(BF)

    def gate_parts(s, first, last):
        def part(p, _):
            gate_part(s, mp ^ p)
            return 0

        lax.fori_loop(first, last, part, 0)

    def send_whole(s, q, may_be_own):
        def one(u, _):
            to = half_k * TH + partner_half(tm, u)
            src, dst = chan.at[s, q, lax.rem(to, TH)], arrived.at[:, tm, 2 * s + chip]

            def away():
                remote(src, dst, a_send.at[0], a_recv.at[0], (to, q)).start()

            if may_be_own:
                pl.when(to != tm)(away)
                pl.when(to == tm)(lambda: pltpu.make_async_copy(src, dst, a_recv.at[0]).start())
            else:
                away()
            return 0

        lax.fori_loop(0, TH, one, 0, unroll=4)

    def send_half(s, q, h, may_be_own):
        def one(u, _):
            to = half_k * TH + partner_half(tm, u)
            src, dst = chan.at[s, q, lax.rem(to, TH), h], arrived.at[h, tm, 2 * s + chip]

            def away():
                remote(src, dst, a_send.at[1 + h], a_recv.at[1 + h], (to, q)).start()

            if may_be_own:
                pl.when(to != tm)(away)
                pl.when(to == tm)(lambda: pltpu.make_async_copy(src, dst, a_recv.at[1 + h]).start())
            else:
                away()
            return 0

        lax.fori_loop(0, TH, one, 0, unroll=4)

    def mix(s, q):
        v = jnp.dot(gated[s], mw[q], preferred_element_type=F32)
        for h in range(2):
            chan[s, q, :, h] = v[:, h * HALF:(h + 1) * HALF].reshape(TH, LB, HALF).astype(BF)

    def mix_and_send(s, first, last):
        if first == 0:
            mix(s, mp)
            send_whole(s, mp, True)
        def part(p, _):
            mix(s, mp ^ p)
            send_whole(s, mp ^ p, False)
            return 0

        lax.fori_loop(max(first, 1), last, part, 0)

    def mix_and_send_half(s):
        mix(s, mp)
        send_half(s, mp, 0, True)

        def part(p, _):
            mix(s, mp ^ p)
            send_half(s, mp ^ p, 0, False)
            return 0

        lax.fori_loop(1, MP, part, 0)

    def send_other_half(s):
        send_half(s, mp, 1, True)

        def part(p, _):
            send_half(s, mp ^ p, 1, False)
            return 0

        lax.fori_loop(1, MP, part, 0)

    def take(s):
        fr[s][0].wait_recv()
        fr[s][2].start()
        if s + 1 < ST:
            fr[s][0].wait_send()
            fr[s + 1][0].start()
            fr[s + 1][1].start()

    def whole(s):
        own[s].wait()
        own[ST + s].wait()
        fr[s][1].wait_recv()
        fr[s][2].wait_recv()

    def gather(last, line, on):
        for n in range(3):
            line[n].wait_recv()
            on[n + 1].start()
        last.wait_recv()
        on[4].start()

    take(0)
    gather(glast, gline, gon)
    glast.wait_send()
    mfirst.start()
    whole(0)
    own[2 * ST].wait()
    gnear.wait_recv()
    gate_parts(0, 0, 2)
    for c in gon:
        c.wait_recv()
    gate_parts(0, 2, MP)
    mfirst.wait_recv()
    for c in (*mline, mon[0]):
        c.start()
    mfirst.wait_send()
    mlast.start()
    own[2 * ST + 1].wait()
    mnear.wait_recv()
    mix_and_send(0, 0, 2)
    take(1)
    whole(1)
    gate_parts(1, 0, MP)
    mix_and_send(1, 0, 2)
    gather(mlast, mline, mon)
    for c in mon:
        c.wait_recv()
    mix_and_send(0, 2, MP)
    mix_and_send(1, 2, MP)
    for s in (2, 3):
        take(s)
        whole(s)
        gate_parts(s, 0, MP)
        mix_and_send_half(s)
    for s in (2, 3):
        send_other_half(s)

    own[2 * ST + 2].wait()
    got = arrived.at[:, :, pl.ds(0, 4)]
    pltpu.make_async_copy(got, got, a_recv.at[0]).wait()
    for h in range(2):
        got = arrived.at[h, :, pl.ds(4, 4)]
        pltpu.make_async_copy(got, got, a_recv.at[1 + h]).wait()

        def widen(n, _):
            t = arrived[h, pl.ds(n * 8, 8)]
            rows[pl.ds(pl.multiple_of(n * 512, 512), 512), :] = t.astype(F32).reshape(512, HALF)
            return 0

        lax.fori_loop(0, 8, widen, 0)
        for k in range(LB):
            v = rows[pl.ds(k, NB, stride=LB), :].astype(BF)
            sums[pl.ds(k, NB, stride=LB), :] = jnp.dot(sv[k], v, preferred_element_type=F32)

        def narrow(n, _):
            t = sums[pl.ds(pl.multiple_of(n * 512, 512), 512), :]
            second[h, pl.ds(n * 8, 8)] = t.reshape(8, LB, LB, HALF).astype(BF)
            return 0

        lax.fori_loop(0, 8, narrow, 0)
        half = pl.ds(h * HALF, HALF)
        pltpu.make_async_copy(second.at[h, tm], out.at[:, tm, :, half], o_recv.at[h]).start()

        def place(u, _):
            to = partner(tm, u)
            remote(second.at[h, to], out.at[:, tm, :, half], o_send.at[h], o_recv.at[h], (to, mp)).start()
            return 0

        lax.fori_loop(1, TM, place, 0, unroll=3)

    for s in range(ST):
        fr[s][1].wait_send()
        fr[s][2].wait_send()
    fr[ST - 1][0].wait_send()
    for c in (gnear, *gline, *gon, mnear, mlast, *mline, *mon):
        c.wait_send()

    def left(src, sem):
        pltpu.make_async_copy(src, src, sem).wait()

    keeps = tm // TH == half_k

    def drop_own(part, sem):
        whole, rest = part(TH), part(TH - 1)
        pl.when(keeps)(lambda: left(rest, sem))
        pl.when(jnp.logical_not(keeps))(lambda: left(whole, sem))

    for s in (0, 1):
        for q in range(1, MP):
            left(chan.at[s, q], a_send.at[0])
        drop_own(lambda n: chan.at[s, 0, pl.ds(0, n)], a_send.at[0])
    for h in range(2):
        for s in (2, 3):
            for q in range(1, MP):
                left(chan.at[s, q, :, h], a_send.at[1 + h])
            drop_own(lambda n: chan.at[s, 0, pl.ds(0, n), h], a_send.at[1 + h])
        left(second.at[h, pl.ds(0, TM - 1)], o_send.at[h])
        half = pl.ds(h * HALF, HALF)
        left(out.at[:, :, :, half], o_recv.at[h])


def on_device(frames, first_factor, second_factor, gate_w, mix_w):
    frames = frames.reshape(LB, NB, DW)
    out = pl.pallas_call(
        kernel,
        out_shape=pltpu.VMEM((LB, TM, LB, DW), BF),
        in_specs=[pl.BlockSpec(memory_space=pltpu.HBM)] * 5,
        out_specs=pl.BlockSpec(memory_space=pl.ANY),
        scratch_shapes=[
            pltpu.VMEM((ST, NB, MP * DW), BF),
            pltpu.VMEM((ST, KH, NB), BF),
            pltpu.VMEM((LB, NB, NB), BF),
            pltpu.VMEM((MP, MP * DW, DW), BF),
            pltpu.VMEM((MP, MP * DW, DW), BF),
            pltpu.VMEM((ST, KH, MP * DW), BF),
            pltpu.VMEM((ST, MP, TH, 2, LB, HALF), BF),
            pltpu.VMEM((2, TM, LB, LB, HALF), BF),
            pltpu.VMEM((NB * LB, HALF), F32),
            pltpu.VMEM((NB * LB, HALF), F32),
            pltpu.VMEM((2, TM, LB, LB, HALF), BF),
            pltpu.SemaphoreType.DMA((2 * ST + 3,)),
            pltpu.SemaphoreType.DMA((ST, 3)),
            pltpu.SemaphoreType.DMA((ST, 3)),
            pltpu.SemaphoreType.DMA((2, 11)),
            pltpu.SemaphoreType.DMA((2, 11)),
            pltpu.SemaphoreType.DMA((3,)),
            pltpu.SemaphoreType.DMA((3,)),
            pltpu.SemaphoreType.DMA((2,)),
            pltpu.SemaphoreType.DMA((2,)),
            pltpu.SemaphoreType.REGULAR((2,)),
        ],
        compiler_params=pltpu.CompilerParams(
            collective_id=0, has_side_effects=True, vmem_limit_bytes=56 << 20),
        cost_estimate=pl.CostEstimate(flops=6_500_000_000, bytes_accessed=16 << 20, transcendentals=1 << 20),
        name="monarch",
    )(frames, first_factor, second_factor, gate_w, mix_w)
    return out.reshape(LB * NB, DW)


def solution(mesh):
    in_specs = (
        P("tm", "mp"),
        P("tm", None, None),
        P("tm", None, None),
        P(None, "mp"),
        P(None, "mp"),
    )
    return jax.shard_map(
        on_device, mesh=mesh, in_specs=in_specs, out_specs=P("tm", "mp"), check_vma=False
    )
```

time: 124 us -> 122 us (0.984); the launches traced: 123 us -> 122 us
  no operation moved by 1% of the time
where the time goes in v3:
time: 122 us
  Pallas kernels  121 us (99%)
  local copies, waits for them, and re-layouts  1.32 us (1%)
    pallas_call x1, Pallas kernels, on_device(): pl.pallas_call(kernel, out_shape=pltpu.VMEM((LB, TM, LB, DW), BF), in_spe...  121 us

profile of v3, /device:TPU:1, one launch (start us, length us, event | category | flops | bytes accessed | tf_op | source)
XLA Modules:
  0.0 122.0 jit_solution(10669551405819625471)
XLA Ops:
  0.0 120.7 %monarch.1 = bf16[8,64,8,256]{3,2,1,0:T(8,128)(2,1)S(1)} custom-call(bf16[8,512,256]{2,1,0:T(8,128)(2,1)} %bitcast.3, bf16[8,512,512]{2,1,0:T(8,128)(2,1)} %first_factor.1, bf16[8,512,512]{2,1,0:T(8,128)(2,1)} %second_factor.1, bf16[1024,256]{1,0:T(8,128)(2,1)} %gate_w.1, bf16[1024,256]{1,0:T(8,128)(2,1)} %mix_w.1), custom_call_target="tpu_custom_call" | custom-call | flops 6499999744 | bytes 16777216 | tf_op jit(solution)/shard_map/monarch/pallas_call | solution.py:319
  120.7 1.3 %copy.7 = bf16[4096,256]{1,0:T(8,128)(2,1)} copy(bf16[4096,256]{1,0:T(8,128)(2,1)S(1)} %bitcast.2) | data formatting | bytes 4194304

commit v4 on v3

--- a/solution.py
+++ b/solution.py
@@ -173,25 +173,27 @@
 
         lax.fori_loop(max(first, 1), last, part, 0)
 
-    def mix_and_send_half(s):
-        mix(s, mp)
-        send_half(s, mp, 0, True)
+    def mixes_and_halves(s, first):
+        if first == 0:
+            mix(s, mp)
+            send_half(s, mp, 0, True)
 
         def part(p, _):
             mix(s, mp ^ p)
             send_half(s, mp ^ p, 0, False)
             return 0
 
-        lax.fori_loop(1, MP, part, 0)
-
-    def send_other_half(s):
-        send_half(s, mp, 1, True)
+        lax.fori_loop(max(first, 1), MP, part, 0)
+
+    def other_halves(s, first):
+        if first == 0:
+            send_half(s, mp, 1, True)
 
         def part(p, _):
             send_half(s, mp ^ p, 1, False)
             return 0
 
-        lax.fori_loop(1, MP, part, 0)
+        lax.fori_loop(max(first, 1), MP, part, 0)
 
     def take(s):
         fr[s][0].wait_recv()
@@ -241,20 +243,22 @@
     for c in mon:
         c.wait_recv()
     mix_and_send(0, 2, MP)
-    mix_and_send(1, 2, MP)
+    mixes_and_halves(1, 2)
     for s in (2, 3):
         take(s)
         whole(s)
         gate_parts(s, 0, MP)
-        mix_and_send_half(s)
+        mixes_and_halves(s, 0)
+        if s == 2:
+            other_halves(1, 2)
     for s in (2, 3):
-        send_other_half(s)
+        other_halves(s, 0)
 
     own[2 * ST + 2].wait()
-    got = arrived.at[:, :, pl.ds(0, 4)]
+    got = arrived.at[:, :, pl.ds(0, 3)]
     pltpu.make_async_copy(got, got, a_recv.at[0]).wait()
     for h in range(2):
-        got = arrived.at[h, :, pl.ds(4, 4)]
+        got = arrived.at[h, :, pl.ds(3, 5)]
         pltpu.make_async_copy(got, got, a_recv.at[1 + h]).wait()
 
         def widen(n, _):
@@ -300,11 +304,13 @@
         pl.when(keeps)(lambda: left(rest, sem))
         pl.when(jnp.logical_not(keeps))(lambda: left(whole, sem))
 
-    for s in (0, 1):
-        for q in range(1, MP):
+    for s, whole_columns in ((0, MP), (1, 2)):
+        for q in range(1, whole_columns):
             left(chan.at[s, q], a_send.at[0])
         drop_own(lambda n: chan.at[s, 0, pl.ds(0, n)], a_send.at[0])
     for h in range(2):
+        for q in range(2, MP):
+            left(chan.at[1, q, :, h], a_send.at[1 + h])
         for s in (2, 3):
             for q in range(1, MP):
                 left(chan.at[s, q, :, h], a_send.at[1 + h])

time: 122 us -> 121 us (level)
  no operation moved by 1% of the time
where the time goes in v4:
time: 121 us
  Pallas kernels  120 us (99%)
  local copies, waits for them, and re-layouts  1.32 us (1%)
    pallas_call x1, Pallas kernels, on_device(): pl.pallas_call(kernel, out_shape=pltpu.VMEM((LB, TM, LB, DW), BF), in_spe...  120 us

profile of v4, /device:TPU:1, one launch (start us, length us, event | category | flops | bytes accessed | tf_op | source)
XLA Modules:
  0.0 121.3 jit_solution(13275788905647923860)
XLA Ops:
  0.0 120.0 %monarch.1 = bf16[8,64,8,256]{3,2,1,0:T(8,128)(2,1)S(1)} custom-call(bf16[8,512,256]{2,1,0:T(8,128)(2,1)} %bitcast.3, bf16[8,512,512]{2,1,0:T(8,128)(2,1)} %first_factor.1, bf16[8,512,512]{2,1,0:T(8,128)(2,1)} %second_factor.1, bf16[1024,256]{1,0:T(8,128)(2,1)} %gate_w.1, bf16[1024,256]{1,0:T(8,128)(2,1)} %mix_w.1), custom_call_target="tpu_custom_call" | custom-call | flops 6499999744 | bytes 16777216 | tf_op jit(solution)/shard_map/monarch/pallas_call | solution.py:325
  120.0 1.3 %copy.7 = bf16[4096,256]{1,0:T(8,128)(2,1)} copy(bf16[4096,256]{1,0:T(8,128)(2,1)S(1)} %bitcast.2) | data formatting | bytes 4194304

commit v5 on v4

--- a/solution.py
+++ b/solution.py
@@ -243,9 +243,11 @@
     for c in mon:
         c.wait_recv()
     mix_and_send(0, 2, MP)
+    take(2)
     mixes_and_halves(1, 2)
     for s in (2, 3):
-        take(s)
+        if s == 3:
+            take(3)
         whole(s)
         gate_parts(s, 0, MP)
         mixes_and_halves(s, 0)

time: 121 us -> 121 us (level)
  no operation moved by 1% of the time
where the time goes in v5:
time: 121 us
  Pallas kernels  119 us (98%)
  local copies, waits for them, and re-layouts  1.32 us (1%)
    pallas_call x1, Pallas kernels, on_device(): pl.pallas_call(kernel, out_shape=pltpu.VMEM((LB, TM, LB, DW), BF), in_spe...  119 us

profile of v5, /device:TPU:1, one launch (start us, length us, event | category | flops | bytes accessed | tf_op | source)
XLA Modules:
  0.0 120.7 jit_solution(14138611068571144167)
XLA Ops:
  0.0 119.4 %monarch.1 = bf16[8,64,8,256]{3,2,1,0:T(8,128)(2,1)S(1)} custom-call(bf16[8,512,256]{2,1,0:T(8,128)(2,1)} %bitcast.3, bf16[8,512,512]{2,1,0:T(8,128)(2,1)} %first_factor.1, bf16[8,512,512]{2,1,0:T(8,128)(2,1)} %second_factor.1, bf16[1024,256]{1,0:T(8,128)(2,1)} %gate_w.1, bf16[1024,256]{1,0:T(8,128)(2,1)} %mix_w.1), custom_call_target="tpu_custom_call" | custom-call | flops 6499999744 | bytes 16777216 | tf_op jit(solution)/shard_map/monarch/pallas_call | solution.py:327
  119.4 1.3 %copy.7 = bf16[4096,256]{1,0:T(8,128)(2,1)} copy(bf16[4096,256]{1,0:T(8,128)(2,1)S(1)} %bitcast.2) | data formatting | bytes 4194304
